TPU v7x, 256 devices: a whole 4x4x8 slice. The times are simulated.
256 devices in a mesh: mem: 16 (over z, core), gx: 4 (over x), gy: 4 (over y).
Axes of the slice: x: 4, y: 4, z: 8, core: 2. Of those that a mesh axis runs over, the one named last changes fastest.
Arguments:
- state: bfloat16 [2048, 128, 4, 256], P(('gx', 'gy'), 'mem'), may hold values from -6 to 6
- obs_ens: float32 [128, 4, 4, 8192], P('mem', 'gx', 'gy'), may hold values from -6 to 6
- obs_values: float32 [2, 4, 4, 8192], P(None, 'gx', 'gy'), may hold values from -4 to 4, as said below
- obs_index: int32 [2048, 128], P(('gx', 'gy')), may hold values from 0 to 67583, as said below
- patch_count: int32 [2048], P(('gx', 'gy')), may hold values from 32 to 128
- slot_weight: float32 [2048, 128], P(('gx', 'gy')), may hold values from 0.05 to 1
Outputs:
- analysis: bfloat16 [2048, 128, 4, 256], P(('gx', 'gy'), 'mem')
Inputs may be any that keep to these rules, and one draw needn't show every extreme that they name: `obs_index`: every tile's list holds 8192 observations. A slot names another tile only at positions below 2048, and never a tile outside the grid. Slots at or beyond a patch's count hold valid codes too. `obs_values`: component 1 is positive.
All inputs are finite; a program needn't handle non-finite values.
Results may differ from a plain program's by a relative error of at most 0.006.
Values may be sent and summed in bfloat16 or wider, within the bound.
A program may use at most 128 MiB of HBM per device.

v0:
```python
import jax
import jax.numpy as jnp
from jax import lax
from jax.sharding import PartitionSpec as P

NS = 6


HIGHEST = lax.Precision.HIGHEST


def padded(block, sides, width):
    for axis, dim in sides:
        count = lax.axis_size(axis)
        forward = [(i, i + 1) for i in range(count - 1)]
        backward = [(target, source) for source, target in forward]
        low = lax.ppermute(
            lax.slice_in_dim(block, block.shape[dim] - width, None, axis=dim), axis, forward
        )
        high = lax.ppermute(lax.slice_in_dim(block, 0, width, axis=dim), axis, backward)
        block = jnp.concatenate([low, block, high], axis=dim)
    return block


def pick_obs(near_pool, indices, obs_len, near_len):
    codes = indices // obs_len
    offsets = indices % obs_len
    near_pos = codes * near_len + jnp.minimum(offsets, near_len - 1)
    from_near = jnp.take(near_pool, near_pos, axis=1)
    return from_near


def patch_weights(chosen, observed, obs_rate, ens_size):
    mean_obs = jnp.mean(chosen, axis=0)
    spread = chosen - mean_obs
    misfit = observed - mean_obs
    gram_mat = jnp.einsum("jps,kps->pjk", spread * obs_rate, spread, precision=HIGHEST)
    identity = jnp.eye(ens_size, dtype=jnp.float32)
    system = gram_mat + (ens_size - 1.0) * identity
    frob_norm = jnp.sqrt(jnp.sum(system * system, axis=(1, 2)))[:, None, None]
    root_est = system / frob_norm
    inverse = jnp.broadcast_to(identity, system.shape)
    for sweep_id in range(NS):
        factor = 1.5 * identity - 0.5 * jnp.einsum(
            "pij,pjk->pik", inverse, root_est, precision=HIGHEST
        )
        root_est = jnp.einsum("pij,pjk->pik", root_est, factor, precision=HIGHEST)
        inverse = jnp.einsum("pij,pjk->pik", factor, inverse, precision=HIGHEST)
    inv_half = inverse / jnp.sqrt(frob_norm)
    covariance = jnp.einsum("pij,pjk->pik", inv_half, inv_half, precision=HIGHEST)
    pulled = jnp.einsum("jps,ps->pj", spread, obs_rate * misfit, precision=HIGHEST)
    mean_shift = jnp.einsum("pjk,pk->pj", covariance, pulled, precision=HIGHEST)
    flipped = jnp.sqrt(ens_size - 1.0) * jnp.swapaxes(inv_half, 1, 2) + mean_shift[:, None, :]
    return flipped.astype(jnp.bfloat16)


def body(state, obs_ens, obs_values, obs_index, patch_count, slot_weight):
    ens_local = obs_ens.shape[0]
    obs_len = obs_ens.shape[3]
    patches_dev = obs_index.shape[0]
    slot_total = obs_index.shape[1]
    share = patches_dev // lax.axis_size("mem")
    first_patch = lax.axis_index("mem") * share
    near_ens, near_val = (
        padded(obs_ens, (("gx", 1), ("gy", 2)), 1),
        padded(obs_values, (("gx", 1), ("gy", 2)), 1),
    )
    chosen = pick_obs(
        near_ens.reshape(ens_local, 9 * obs_len), obs_index.reshape(-1), obs_len, obs_len
    )
    chosen = chosen.reshape(ens_local, patches_dev, slot_total)
    gathered = lax.all_to_all(chosen, "mem", split_axis=1, concat_axis=0, tiled=True)
    own_index = lax.dynamic_slice_in_dim(obs_index, first_patch, share, 0)
    picked = pick_obs(near_val.reshape(2, 9 * obs_len), own_index.reshape(-1), obs_len, obs_len)
    picked = picked.reshape(2, share, slot_total)
    counts = lax.dynamic_slice_in_dim(patch_count, first_patch, share, 0)
    weights = lax.dynamic_slice_in_dim(slot_weight, first_patch, share, 0)
    slot_ids = jnp.arange(slot_total, dtype=jnp.int32)
    obs_rate = picked[1] * weights * (slot_ids[None, :] < counts[:, None]).astype(jnp.float32)
    flipped = patch_weights(gathered, picked[0], obs_rate, gathered.shape[0])
    received = lax.all_to_all(state, "mem", split_axis=0, concat_axis=1, tiled=True)
    patch_num, ens_all, lev_num, col_num = received.shape
    widened = received.astype(jnp.float32)
    mean_state = jnp.mean(widened, axis=1, keepdims=True)
    perturb = (
        (widened - mean_state).astype(jnp.bfloat16).reshape(patch_num, ens_all, lev_num * col_num)
    )
    mixed_sum = jnp.einsum("pkj,pjx->pkx", flipped, perturb, preferred_element_type=jnp.float32)
    updated = (mixed_sum.reshape(patch_num, ens_all, lev_num, col_num) + mean_state).astype(
        jnp.bfloat16
    )
    return lax.all_to_all(updated, "mem", split_axis=1, concat_axis=0, tiled=True)


def solution(mesh):
    placed = (
        P(("gx", "gy"), "mem", None, None),
        P("mem", "gx", "gy", None),
        P(None, "gx", "gy", None),
        P(("gx", "gy"), None),
        P(("gx", "gy")),
        P(("gx", "gy"), None),
    )
    return jax.shard_map(
        body,
        mesh=mesh,
        in_specs=placed,
        out_specs=P(("gx", "gy"), "mem", None, None),
        check_vma=False,
    )
```

profile of v0, /device:TPU:65, one launch (start us, length us, event | category | flops | bytes accessed | tf_op | source)
XLA Modules:
  0.0 306.8 jit_solution(7027827829225124338)
XLA Ops:
  0.0 3.1 %collective-permute-start.4 = (f32[2,1,1,8192]{3,2,1,0:T(1,128)}, f32[2,1,1,8192]{3,2,1,0:T(1,128)S(1)}, u32[]{:S(2)}, u32[]{:S(2)}) collective-permute-start(f32[2,1,1,8192]{3,2,1,0:T(1,128)} %param.8), channel_id=1, source_target_pairs={{0,4},{4,8},{8,12},{1,5},{5,9},{9,13},{2,6},{6,10},{10,14},{3,7},{... | collective-permute-start | bytes 196616 | tf_op jit(solution)/shard_map/ppermute | solution.py:17
  3.1 1.3 collective-permute-start.5
  4.4 4.0 %collective-permute-start = (f32[8,1,1,8192]{3,2,1,0:T(1,128)}, f32[8,1,1,8192]{3,2,1,0:T(1,128)S(1)}, u32[]{:S(2)}, u32[]{:S(2)}) collective-permute-start(f32[8,1,1,8192]{3,2,1,0:T(1,128)} %param.7), channel_id=1, source_target_pairs={{0,4},{4,8},{8,12},{1,5},{5,9},{9,13},{2,6},{6,10},{10,14},{3,7},{... | collective-permute-start | bytes 786440 | tf_op jit(solution)/shard_map/ppermute | solution.py:17
  8.4 1.3 collective-permute-start.1
  9.8 0.9 compare_and_fusion
  10.7 1.3 compare_and_fusion.1
  12.6 1.4 compare_select_fusion
  14.1 1.2 dynamic_slice.9
  16.0 0.9 constant_dynamic-update-slice_fusion.4
  16.8 1.0 constant_dynamic-update-slice_fusion.1
  17.9 3.2 %collective-permute-start.2 = (f32[8,3,1,8192]{3,2,1,0:T(1,128)S(1)}, f32[8,3,1,8192]{3,2,1,0:T(1,128)S(1)}, u32[]{:S(2)}, u32[]{:S(2)}) collective-permute-start(f32[8,3,1,8192]{3,2,1,0:T(1,128)S(1)} %constant_dynamic-update-slice_fusion), channel_id=1, source_target_pairs={{0,1},{1,2},{2,3},{4,5},{5,6},{6,7},{8,9},{9,10},{10,11},{12,13},{... | collective-permute-start | bytes 2359304 | tf_op jit(solution)/shard_map/ppermute | solution.py:17
  21.1 1.3 collective-permute-start.3
  22.5 4.7 %collective-permute-start.6 = (f32[2,3,1,8192]{3,2,1,0:T(1,128)S(1)}, f32[2,3,1,8192]{3,2,1,0:T(1,128)}, u32[]{:S(2)}, u32[]{:S(2)}) collective-permute-start(f32[2,3,1,8192]{3,2,1,0:T(1,128)S(1)} %constant_dynamic-update-slice_fusion.3), channel_id=1, source_target_pairs={{0,1},{1,2},{2,3},{4,5},{5,6},{6,7},{8,9},{9,10},{10,11},{12,13},{... | collective-permute-start | bytes 589832 | tf_op jit(solution)/shard_map/ppermute | solution.py:17
  27.1 1.3 collective-permute-start.7
  28.4 8.0 %collective-permute-done.2 = f32[8,3,1,8192]{3,2,1,0:T(1,128)S(1)} collective-permute-done((f32[8,3,1,8192]{3,2,1,0:T(1,128)S(1)}, f32[8,3,1,8192]{3,2,1,0:T(1,128)S(1)}, u32[]{:S(2)}, u32[]{:S(2)}) %collective-permute-start.2) | collective-permute-done | bytes 786464 | tf_op jit(solution)/shard_map/ppermute | solution.py:17
  36.4 3.9 %collective-permute-done.3 = f32[8,3,1,8192]{3,2,1,0:T(1,128)S(1)} collective-permute-done((f32[8,3,1,8192]{3,2,1,0:T(1,128)S(1)}, f32[8,3,1,8192]{3,2,1,0:T(1,128)S(1)}, u32[]{:S(2)}, u32[]{:S(2)}) %collective-permute-start.3) | collective-permute-done | bytes 786464 | tf_op jit(solution)/shard_map/ppermute | solution.py:20
  40.3 2.3 pad_maximum_fusion
  42.6 18.2 %copy.46 = f32[8,3,3,8192]{0,3,2,1:T(8,128)} copy(f32[8,3,3,8192]{3,2,1,0:T(4,128)S(1)} %pad_maximum_fusion) | data formatting | bytes 4718592 | tf_op jit(solution)/shard_map/concatenate | solution.py:21
  60.7 66.1 %gather_fusion = f32[16384,8]{1,0:T(8,128)} fusion(f32[8,73728]{0,1:T(8,128)} %bitcast.111, s32[16384]{0:T(1024)S(1)} %broadcast_clamp_fusion), kind=kCustom, calls=%fused_computation | custom fusion | bytes 1114112 | tf_op jit(solution)/shard_map/jit(_take)/gather | solution.py:29
  126.8 5.4 %copy.47 = f32[8,128,128]{2,0,1:T(8,128)S(1)} copy(f32[8,128,128]{0,2,1:T(8,128)} %bitcast.118) | data formatting | bytes 1048576 | tf_op jit(solution)/shard_map/jit(_take)/gather | solution.py:29
  132.2 0.9 broadcast_select_fusion
  133.1 12.6 %all-to-all-start = ((f32[8,128,128]{2,0,1:T(8,128)}), f32[8,128,128]{2,0,1:T(8,128)S(1)}, u32[]{:S(2)}, u32[]{:S(2)}) async-start(f32[8,128,128]{2,0,1:T(8,128)} %broadcast_select_fusion), calls=%async_computation | async-start | bytes 1048576 | tf_op jit(solution)/shard_map/all_to_all | solution.py:72
  145.7 1.6 pad_maximum_fusion.1
  147.3 17.1 %copy.49 = f32[2,3,3,8192]{0,3,2,1:T(8,128)} copy(f32[2,3,3,8192]{3,2,1,0:T(4,128)S(1)} %pad_maximum_fusion.1) | data formatting | bytes 1179648 | tf_op jit(solution)/shard_map/concatenate | solution.py:21
  164.4 14.5 %gather_fusion.1 = f32[1024,2]{1,0:T(8,128)S(1)} fusion(f32[2,73728]{0,1:T(8,128)} %bitcast.112, s32[1024]{0:T(1024)S(1)} %copy-done.1), kind=kCustom, calls=%fused_computation.1 | custom fusion | bytes 20480 | tf_op jit(solution)/shard_map/jit(_take)/gather | solution.py:29
  179.7 7.2 %all-to-all-start.1 = ((bf16[128,8,4,256]{3,2,1,0:T(4,128)(2,1)}), bf16[128,8,4,256]{3,2,1,0:T(4,128)(2,1)S(1)}, u32[]{:S(2)}, u32[]{:S(2)}) async-start(bf16[128,8,4,256]{3,2,1,0:T(4,128)(2,1)} %param.6), calls=%async_computation.1 | async-start | bytes 4194304 | tf_op jit(solution)/shard_map/all_to_all | solution.py:81
  187.0 0.8 fusion.36
  187.7 1.3 multiply_reduce_fusion
  189.1 0.7 fusion.8
  189.7 0.7 fusion.18
  191.0 0.9 convolution_bitcast_fusion
  191.9 0.7 fusion.7
  192.6 0.6 fusion.46
  193.9 0.6 fusion.6
  194.6 0.6 fusion.48
  195.9 0.6 fusion.5
  197.9 0.6 fusion.4
  199.8 0.9 fusion.3
  202.0 0.9 fusion.54
  202.9 31.5 %all-to-all-done.1 = bf16[128,8,4,256]{3,2,1,0:T(4,128)(2,1)S(1)} async-done(((bf16[128,8,4,256]{3,2,1,0:T(4,128)(2,1)}), bf16[128,8,4,256]{3,2,1,0:T(4,128)(2,1)S(1)}, u32[]{:S(2)}, u32[]{:S(2)}) %all-to-all-start.1) | async-done | bytes 2097184 | tf_op jit(solution)/shard_map/all_to_all | solution.py:81
  234.4 1.4 convert_reduce_fusion
  235.9 0.7 convert_element_type.46
  236.6 1.0 copy.50
  237.6 2.8 fusion.1
  240.4 5.6 %reshape.314 = f32[8,128,4,256]{3,2,1,0:T(4,128)} reshape(f32[8,128,1024]{2,1,0:T(8,128)} %fusion.1) | data formatting | bytes 8388608 | tf_op jit(solution)/shard_map/reshape | solution.py:89
  246.0 3.4 %fusion = bf16[8,128,4,256]{3,2,0,1:T(4,128)(2,1)S(1)} fusion(f32[8,128,4,256]{3,2,1,0:T(4,128)} %reshape.314, f32[8,4,256]{2,1,0:T(4,128)S(1)} %copy.54), kind=kLoop, calls=%fused_computation.3 | loop fusion | flops 2097152 | bytes 6324224 | tf_op jit(solution)/shard_map/convert_element_type | solution.py:89
  249.4 54.8 %all_to_all.45 = bf16[8,128,4,256]{3,2,0,1:T(4,128)(2,1)S(1)} all-to-all(bf16[8,128,4,256]{3,2,0,1:T(4,128)(2,1)S(1)} %fusion), channel_id=1, replica_groups=mesh['mem'=16,'gx'=4,'gy'=4] {'mem'}, dimensions={1} | all-to-all | bytes 4194304 | tf_op jit(solution)/shard_map/all_to_all | solution.py:92
  304.3 2.5 copy.56
  (41 shorter events, 8.0 us)
Async XLA Ops:
  0.0 15.9 %collective-permute-start.4 = (f32[2,1,1,8192]{3,2,1,0:T(1,128)}, f32[2,1,1,8192]{3,2,1,0:T(1,128)S(1)}, u32[]{:S(2)}, u32[]{:S(2)}) collective-permute-start(f32[2,1,1,8192]{3,2,1,0:T(1,128)} %param.8), channel_id=1, source_target_pairs={{0,4},{4,8},{8,12},{1,5},{5,9},{9,13},{2,6},{6,10},{10,14},{3,7},{... | collective-permute-start | bytes 196616 | tf_op jit(solution)/shard_map/ppermute | solution.py:17
  3.1 19.3 %collective-permute-start.5 = (f32[2,1,1,8192]{3,2,1,0:T(1,128)}, f32[2,1,1,8192]{3,2,1,0:T(1,128)S(1)}, u32[]{:S(2)}, u32[]{:S(2)}) collective-permute-start(f32[2,1,1,8192]{3,2,1,0:T(1,128)} %param.8), channel_id=1, source_target_pairs={{4,0},{8,4},{12,8},{5,1},{9,5},{13,9},{6,2},{10,6},{14,10},{7,3},{... | collective-permute-start | bytes 196616 | tf_op jit(solution)/shard_map/ppermute | solution.py:20
  4.4 12.4 %collective-permute-start = (f32[8,1,1,8192]{3,2,1,0:T(1,128)}, f32[8,1,1,8192]{3,2,1,0:T(1,128)S(1)}, u32[]{:S(2)}, u32[]{:S(2)}) collective-permute-start(f32[8,1,1,8192]{3,2,1,0:T(1,128)} %param.7), channel_id=1, source_target_pairs={{0,4},{4,8},{8,12},{1,5},{5,9},{9,13},{2,6},{6,10},{10,14},{3,7},{... | collective-permute-start | bytes 786440 | tf_op jit(solution)/shard_map/ppermute | solution.py:17
  8.4 9.4 %collective-permute-start.1 = (f32[8,1,1,8192]{3,2,1,0:T(1,128)}, f32[8,1,1,8192]{3,2,1,0:T(1,128)S(1)}, u32[]{:S(2)}, u32[]{:S(2)}) collective-permute-start(f32[8,1,1,8192]{3,2,1,0:T(1,128)} %param.7), channel_id=1, source_target_pairs={{4,0},{8,4},{12,8},{5,1},{9,5},{13,9},{6,2},{10,6},{14,10},{7,3},{... | collective-permute-start | bytes 786440 | tf_op jit(solution)/shard_map/ppermute | solution.py:20
  17.9 18.5 %collective-permute-start.2 = (f32[8,3,1,8192]{3,2,1,0:T(1,128)S(1)}, f32[8,3,1,8192]{3,2,1,0:T(1,128)S(1)}, u32[]{:S(2)}, u32[]{:S(2)}) collective-permute-start(f32[8,3,1,8192]{3,2,1,0:T(1,128)S(1)} %constant_dynamic-update-slice_fusion), channel_id=1, source_target_pairs={{0,1},{1,2},{2,3},{4,5},{5,6},{6,7},{8,9},{9,10},{10,11},{12,13},{... | collective-permute-start | bytes 2359304 | tf_op jit(solution)/shard_map/ppermute | solution.py:17
  21.1 19.1 %collective-permute-start.3 = (f32[8,3,1,8192]{3,2,1,0:T(1,128)S(1)}, f32[8,3,1,8192]{3,2,1,0:T(1,128)S(1)}, u32[]{:S(2)}, u32[]{:S(2)}) collective-permute-start(f32[8,3,1,8192]{3,2,1,0:T(1,128)S(1)} %constant_dynamic-update-slice_fusion), channel_id=1, source_target_pairs={{1,0},{2,1},{3,2},{5,4},{6,5},{7,6},{9,8},{10,9},{11,10},{13,12},{... | collective-permute-start | bytes 2359304 | tf_op jit(solution)/shard_map/ppermute | solution.py:20
  22.5 123.2 %collective-permute-start.6 = (f32[2,3,1,8192]{3,2,1,0:T(1,128)S(1)}, f32[2,3,1,8192]{3,2,1,0:T(1,128)}, u32[]{:S(2)}, u32[]{:S(2)}) collective-permute-start(f32[2,3,1,8192]{3,2,1,0:T(1,128)S(1)} %constant_dynamic-update-slice_fusion.3), channel_id=1, source_target_pairs={{0,1},{1,2},{2,3},{4,5},{5,6},{6,7},{8,9},{9,10},{10,11},{12,13},{... | collective-permute-start | bytes 589832 | tf_op jit(solution)/shard_map/ppermute | solution.py:17
  27.1 118.5 %collective-permute-start.7 = (f32[2,3,1,8192]{3,2,1,0:T(1,128)S(1)}, f32[2,3,1,8192]{3,2,1,0:T(1,128)}, u32[]{:S(2)}, u32[]{:S(2)}) collective-permute-start(f32[2,3,1,8192]{3,2,1,0:T(1,128)S(1)} %constant_dynamic-update-slice_fusion.3), channel_id=1, source_target_pairs={{1,0},{2,1},{3,2},{5,4},{6,5},{7,6},{9,8},{10,9},{11,10},{13,12},{... | collective-permute-start | bytes 589832 | tf_op jit(solution)/shard_map/ppermute | solution.py:20
  133.1 46.6 %all-to-all-start = ((f32[8,128,128]{2,0,1:T(8,128)}), f32[8,128,128]{2,0,1:T(8,128)S(1)}, u32[]{:S(2)}, u32[]{:S(2)}) async-start(f32[8,128,128]{2,0,1:T(8,128)} %broadcast_select_fusion), calls=%async_computation | async-start | bytes 1048576 | tf_op jit(solution)/shard_map/all_to_all | solution.py:72
  147.3 17.1 %copy-start.1 = (s32[1024]{0:T(1024)S(1)}, s32[1024]{0:T(1024)}, u32[]{:S(2)}) copy-start(s32[1024]{0:T(1024)} %broadcast_clamp_fusion.1) | copy-start | bytes 12292
  147.3 31.7 %copy-start.2 = (pred[1024]{0:T(1024)(128)(4,1)S(1)}, pred[1024]{0:T(1024)(128)(4,1)}, u32[]{:S(2)}) copy-start(pred[1024]{0:T(1024)(128)(4,1)} %get-tuple-element.9) | copy-start | bytes 3076
  164.4 22.6 %copy-start.3 = (s32[8]{0:T(128)S(1)}, s32[8]{0:T(128)}, u32[]{:S(2)}) copy-start(s32[8]{0:T(128)} %dynamic_slice.9) | copy-start | bytes 100
  178.9 10.1 %copy-start = (f32[128,128]{1,0:T(8,128)S(1)}, f32[128,128]{1,0:T(8,128)}, u32[]{:S(2)}) copy-start(f32[128,128]{1,0:T(8,128)} %fusion.27) | copy-start | bytes 196612
  179.7 54.8 %all-to-all-start.1 = ((bf16[128,8,4,256]{3,2,1,0:T(4,128)(2,1)}), bf16[128,8,4,256]{3,2,1,0:T(4,128)(2,1)S(1)}, u32[]{:S(2)}, u32[]{:S(2)}) async-start(bf16[128,8,4,256]{3,2,1,0:T(4,128)(2,1)} %param.6), calls=%async_computation.1 | async-start | bytes 4194304 | tf_op jit(solution)/shard_map/all_to_all | solution.py:81
where the time goes:
time: 312 us; the launch traced here: 307 us
  local copies, waits for them, and re-layouts  134 us (43%)
  blocking collectives  54.8 us (18%)
  waiting for transfers between devices  43.4 us (14%)
  starting transfers between devices  40 us (13%)
  matrix products  17.8 us (6%)
  other arithmetic  16.1 us (5%)
    gather x3, local copies, waits for them, and re-layouts, pick_obs(): from_near = jnp.take(near_pool, near_pos, axis=1)  86 us
    all_to_all x1, blocking collectives, body(): lax.all_to_all(updated, 'mem', split_axis=1, concat_axis=0, tiled=True)  54.8 us
    concatenate x4, local copies, waits for them, and re-layouts, padded(): block = jnp.concatenate([low, block, high], axis=dim)  35.3 us
    all_to_all x1, waiting for transfers between devices, body(): lax.all_to_all(state, 'mem', split_axis=0, concat_axis=1, tiled=True)  31.5 us
    ppermute x4, starting transfers between devices, padded(): lax.ppermute(lax.slice_in_dim(block, block.shape[dim] - width, None, axis...  15 us
    all_to_all x1, starting transfers between devices, body(): lax.all_to_all(chosen, 'mem', split_axis=1, concat_axis=0, tiled=True)  12.6 us
    ppermute x4, waiting for transfers between devices, padded(): lax.ppermute(lax.slice_in_dim(block, block.shape[dim] - width, None, axis...  7.97 us
    all_to_all x1, starting transfers between devices, body(): lax.all_to_all(state, 'mem', split_axis=0, concat_axis=1, tiled=True)  7.24 us
  transfers between devices with their start and end apart: 10, of which 3 were waited for; matrix products, arithmetic and copies ran while one was open for 49% of the time, Pallas kernels for 0%

commit v1 on v0

v1 whole, which is shorter than its diff:
```python
import math

import jax
import jax.numpy as jnp
from jax import lax
from jax.experimental import pallas as pl
from jax.experimental.pallas import tpu as pltpu
from jax.sharding import PartitionSpec as P

NS = 6
MESH = pl.DeviceIdType.MESH
F32 = jnp.float32
BF16 = jnp.bfloat16

GROUP = 16
SHARE = 8
SLOTS = 128
ENS = GROUP * SHARE
PATCHES = GROUP * SHARE
OBS = 8192
RIM = 2048
CHUNK = 256
OWN_CHUNKS = OBS // CHUNK
RIM_CHUNKS = RIM // CHUNK
CHUNKS = OWN_CHUNKS + 8 * RIM_CHUNKS
MSG = SHARE * SHARE + 2 * SHARE
EARLY = 3

SIDES = [(dx, dy) for dx in (-1, 0, 1) for dy in (-1, 0, 1) if (dx, dy) != (0, 0)]


def split(a):
    high = a.astype(BF16)
    return high, (a - high.astype(F32)).astype(BF16)


def mm(a, b):
    a_high, a_low = split(a)
    b_high, b_low = split(b)
    row = jnp.concatenate([b_high, b_low], axis=1)
    out = jnp.dot(
        jnp.concatenate([a_high, a_low], axis=1),
        jnp.concatenate([row, row], axis=0),
        preferred_element_type=F32,
    )
    width = b.shape[1]
    return out[:, :width] + out[:, width:]


def mm_t(a, b):
    a_high, a_low = split(a)
    b_high, b_low = split(b)
    out = lax.dot_general(
        jnp.concatenate([a_high, a_low], axis=1),
        jnp.concatenate(
            [
                jnp.concatenate([b_high, b_high], axis=1),
                jnp.concatenate([b_low, b_low], axis=1),
            ],
            axis=0,
        ),
        (((1,), (1,)), ((), ())),
        preferred_element_type=F32,
    )
    width = b.shape[0]
    return out[:, :width] + out[:, width:]


def kernel(
    state, ens, vals, index, counts, weights, out,
    ens_raw, vals_raw, ens_rim, vals_rim, index_v, weights_v, counts_v,
    pool, mean_f, mean_pool, val_pool, obs_own, rate_own,
    msg_out, msg_in, state_in, root, pulled_s, frob_s, trans, wide, mixed, back,
    local_sem, rim_send, rim_recv, val_send, val_recv,
    msg_send, msg_recv, msg_own, state_send, state_recv, state_own,
    back_send, back_recv, back_own,
):
    me = lax.axis_index("mem")
    tile_x = lax.axis_index("gx")
    tile_y = lax.axis_index("gy")

    loads = [
        pltpu.make_async_copy(ens, ens_raw, local_sem.at[0]),
        pltpu.make_async_copy(vals, vals_raw, local_sem.at[1]),
        pltpu.make_async_copy(index, index_v, local_sem.at[2]),
        pltpu.make_async_copy(
            weights.at[pl.ds(pl.multiple_of(me * SHARE, SHARE), SHARE)],
            weights_v, local_sem.at[3],
        ),
        pltpu.make_async_copy(counts, counts_v, local_sem.at[4]),
    ]

    def tile_at(dx, dy):
        return {
            "gx": lax.rem(tile_x + dx + 4, 4),
            "gy": lax.rem(tile_y + dy + 4, 4),
        }

    barrier = pltpu.get_barrier_semaphore()
    for dx, dy in SIDES:
        pl.semaphore_signal(barrier, inc=1, device_id=tile_at(dx, dy), device_id_type=MESH)
    for step in range(1, GROUP):
        pl.semaphore_signal(
            barrier, inc=1, device_id={"mem": lax.rem(me + step, GROUP)}, device_id_type=MESH
        )
    for load in loads:
        load.start()

    def own_state(patch):
        return pltpu.make_async_copy(
            state.at[me * SHARE + patch], state_in.at[patch, me], state_own.at[patch]
        )

    def send_state(patch):
        def one(step, carry):
            to = lax.rem(me + 5 * step, GROUP)
            pltpu.make_async_remote_copy(
                src_ref=state.at[to * SHARE + patch],
                dst_ref=state_in.at[patch, me],
                send_sem=state_send,
                recv_sem=state_recv.at[patch],
                device_id={"mem": to},
                device_id_type=MESH,
            ).start()
            return carry

        lax.fori_loop(1, GROUP, one, 0)

    for patch in range(SHARE):
        own_state(patch).start()
    pl.semaphore_wait(barrier, len(SIDES) + GROUP - 1)

    loads[0].wait()
    loads[1].wait()
    rims = []
    for side, (dx, dy) in enumerate(SIDES):
        slot = len(SIDES) - 1 - side
        for src, dst, send, recv in (
            (ens_raw, ens_rim, rim_send, rim_recv),
            (vals_raw, vals_rim, val_send, val_recv),
        ):
            copy = pltpu.make_async_remote_copy(
                src_ref=src.at[:, :, :, pl.ds(0, RIM)],
                dst_ref=dst.at[slot],
                send_sem=send.at[slot],
                recv_sem=recv.at[slot],
                device_id=tile_at(dx, dy),
                device_id_type=MESH,
            )
            copy.start()
            rims.append(copy)

    for patch in range(EARLY):
        send_state(patch)

    def fill(chunk_pair, ens_block, vals_block):
        mean = jnp.mean(ens_block, axis=0, keepdims=True)
        dev = ens_block - mean
        rows = pl.ds(pl.multiple_of(chunk_pair * 16, 16), 16)
        pool[rows, :] = jnp.concatenate([dev[:, :CHUNK], dev[:, CHUNK:]], axis=0).astype(BF16)
        mean_f[pl.ds(chunk_pair * 2, 1), :] = mean[:, :CHUNK]
        mean_f[pl.ds(chunk_pair * 2 + 1, 1), :] = mean[:, CHUNK:]
        first = vals_block.astype(BF16).astype(F32)
        rest = vals_block - first
        second = rest.astype(BF16).astype(F32)
        parts = jnp.concatenate([first, second, rest - second, jnp.zeros_like(first)], axis=0)
        val_pool[rows, :] = jnp.concatenate(
            [parts[:, :CHUNK], parts[:, CHUNK:]], axis=0
        ).astype(BF16)

    def fill_own(pair, carry):
        cols = pl.ds(pl.multiple_of(pair * 2 * CHUNK, 2 * CHUNK), 2 * CHUNK)
        fill(
            pair,
            jnp.concatenate([ens_raw[m, 0, :, cols] for m in range(SHARE)], axis=0),
            jnp.concatenate([vals_raw[c, 0, :, cols] for c in range(2)], axis=0),
        )
        return carry

    lax.fori_loop(0, OWN_CHUNKS // 2, fill_own, 0)

    for copy in rims:
        copy.wait()

    def fill_rim(step, carry):
        side = step // (RIM_CHUNKS // 2)
        pair = step % (RIM_CHUNKS // 2)
        cols = pl.ds(pl.multiple_of(pair * 2 * CHUNK, 2 * CHUNK), 2 * CHUNK)
        fill(
            OWN_CHUNKS // 2 + step,
            jnp.concatenate([ens_rim[side, m, 0, :, cols] for m in range(SHARE)], axis=0),
            jnp.concatenate([vals_rim[side, c, 0, :, cols] for c in range(2)], axis=0),
        )
        return carry

    lax.fori_loop(0, 8 * RIM_CHUNKS // 2, fill_rim, 0)
    means = mean_f[...]
    mean_high, mean_low = split(means)
    mean_pool[0:CHUNKS, :] = mean_high
    mean_pool[CHUNKS : 2 * CHUNKS, :] = mean_low

    for load in loads[2:]:
        load.wait()

    sub_iota = lax.broadcasted_iota(jnp.int32, (CHUNK, 2 * SLOTS), 0)
    row_iota = lax.broadcasted_iota(jnp.int32, (8, 2 * SLOTS), 0)

    def pick(table, chunk_of, onehot):
        found = jnp.zeros((8, 2 * SLOTS), F32)
        for block in range(CHUNKS // 16):
            rows = jnp.dot(
                table[block * 128 : (block + 1) * 128, :], onehot, preferred_element_type=F32
            )
            for c in range(16):
                found = jnp.where(chunk_of == block * 16 + c, rows[8 * c : 8 * c + 8], found)
        return found

    def gather(step, carry):
        to = lax.rem(me + 5 * (step + 1), GROUP)
        codes = index_v[pl.ds(pl.multiple_of(to * SHARE, SHARE), SHARE), :]
        tile = codes >> 13
        pos = codes & (OBS - 1)
        side = jnp.where(tile > 4, tile - 1, tile)
        chunk = jnp.where(tile == 4, pos >> 8, OWN_CHUNKS + side * RIM_CHUNKS + (pos >> 8))
        lane = pos & (CHUNK - 1)
        pairs = []
        for pair in range(SHARE // 2):
            two = lambda a: jnp.concatenate(
                [a[2 * pair : 2 * pair + 1], a[2 * pair + 1 : 2 * pair + 2]], axis=1
            )
            onehot = jnp.where(sub_iota == two(lane), 1.0, 0.0).astype(BF16)
            pairs.append((onehot, jnp.broadcast_to(two(chunk), (8, 2 * SLOTS))))
        heads = ([], [])
        for pair, (onehot, chunk_of) in enumerate(pairs):
            dev = pick(pool, chunk_of, onehot)
            msg_out[step, 16 * pair : 16 * pair + 16, :] = jnp.concatenate(
                [dev[:, :SLOTS], dev[:, SLOTS:]], axis=0
            ).astype(BF16)
            rows = jnp.dot(mean_pool[...], onehot, preferred_element_type=F32)
            turned = chunk_of - row_iota
            for part in range(2):
                found = jnp.zeros((8, 2 * SLOTS), F32)
                for k in range(CHUNKS // 8):
                    at = part * CHUNKS + 8 * k
                    found = jnp.where(turned == 8 * k, rows[at : at + 8], found)
                found = jnp.sum(found, axis=0, keepdims=True)
                heads[part].extend([found[:, :SLOTS], found[:, SLOTS:]])
        msg_out[step, SHARE * SHARE : MSG, :] = jnp.concatenate(
            heads[0] + heads[1], axis=0
        ).astype(BF16)

        @pl.when(step < GROUP - 1)
        def _():
            pltpu.make_async_remote_copy(
                src_ref=msg_out.at[step],
                dst_ref=msg_in.at[me],
                send_sem=msg_send,
                recv_sem=msg_recv,
                device_id={"mem": to},
                device_id_type=MESH,
            ).start()

        @pl.when(step == GROUP - 1)
        def _():
            pltpu.make_async_copy(msg_out.at[step], msg_in.at[me], msg_own).start()
            for pair, (onehot, chunk_of) in enumerate(pairs):
                got = pick(val_pool, chunk_of, onehot)
                got = got[0:2] + got[2:4] + got[4:6]
                obs_own[2 * pair : 2 * pair + 1, :] = got[0:1, :SLOTS]
                obs_own[2 * pair + 1 : 2 * pair + 2, :] = got[0:1, SLOTS:]
                rate_own[2 * pair : 2 * pair + 1, :] = got[1:2, :SLOTS]
                rate_own[2 * pair + 1 : 2 * pair + 2, :] = got[1:2, SLOTS:]

        return carry

    lax.fori_loop(0, GROUP, gather, 0)

    for patch in range(EARLY, SHARE):
        send_state(patch)

    msg_all = pltpu.make_async_remote_copy(
        src_ref=msg_out.at[pl.ds(0, GROUP - 1)],
        dst_ref=msg_in.at[pl.ds(0, GROUP - 1)],
        send_sem=msg_send,
        recv_sem=msg_recv,
        device_id={"mem": lax.rem(me + 1, GROUP)},
        device_id_type=MESH,
    )
    msg_all.wait_recv()
    pltpu.make_async_copy(msg_out.at[GROUP - 1], msg_in.at[me], msg_own).wait()

    eye = jnp.where(
        lax.broadcasted_iota(jnp.int32, (ENS, ENS), 0)
        == lax.broadcasted_iota(jnp.int32, (ENS, ENS), 1),
        1.0,
        0.0,
    ).astype(F32)
    lane_iota = lax.broadcasted_iota(jnp.int32, (1, SLOTS), 1)
    counts_row = counts_v[...].reshape(1, PATCHES).astype(F32)
    for p in range(SHARE):
        dev = msg_in[:, SHARE * p : SHARE * p + SHARE, :].astype(F32)
        heads = msg_in[:, SHARE * SHARE : MSG, :].astype(F32)
        head = heads[:, p : p + 1, :] + heads[:, SHARE + p : SHARE + p + 1, :]
        chosen = (dev + head).reshape(ENS, SLOTS)
        mean_obs = jnp.mean(chosen, axis=0, keepdims=True)
        spread = chosen - mean_obs
        count = jnp.sum(
            jnp.where(lane_iota == me * SHARE + p, counts_row, 0.0), axis=1, keepdims=True
        )
        used = lane_iota.astype(F32) < count
        rate = jnp.where(used, rate_own[p : p + 1, :] * weights_v[p : p + 1, :], 0.0)
        misfit = obs_own[p : p + 1, :] - mean_obs
        system = mm_t(spread * rate, spread) + (ENS - 1.0) * eye
        square = jnp.sum(system * system, axis=1, keepdims=True)
        frob = jnp.sqrt(jnp.sum(square, axis=0, keepdims=True))
        pulled_s[p] = mm_t(jnp.broadcast_to(rate * misfit, (8, SLOTS)), spread)
        frob_s[p] = jnp.broadcast_to(frob, (8, SLOTS))
        scaled = system / frob
        change = 0.5 * (eye - scaled)
        root[p, :ENS] = eye + change
        root[p, ENS:] = scaled + mm(scaled, change)

    def sweep(step, carry):
        for p in range(SHARE):
            both = root[p]
            change = 0.5 * (eye - mm(both[:ENS], both[ENS:]))
            root[p] = both + mm(both, change)
        return carry

    lax.fori_loop(1, NS - 1, sweep, 0)
    for p in range(SHARE):
        both = root[p]
        inverse = both[:ENS]
        change = 0.5 * (eye - mm(inverse, both[ENS:]))
        inverse = inverse + mm(inverse, change)
        inv_half = inverse / jnp.sqrt(frob_s[p][0:1, :])
        shift = mm(mm(pulled_s[p], inv_half), inv_half)[0:1]
        trans[p] = (math.sqrt(ENS - 1.0) * inv_half + shift).astype(BF16)

    def analyse(p, carry):
        pltpu.make_async_remote_copy(
            src_ref=state.at[pl.ds(0, GROUP - 1)],
            dst_ref=state_in.at[p, pl.ds(0, GROUP - 1)],
            send_sem=state_send,
            recv_sem=state_recv.at[p],
            device_id={"mem": lax.rem(me + 1, GROUP)},
            device_id_type=MESH,
        ).wait_recv()
        own_state(p).wait()

        def widen(source, carry):
            for m in range(SHARE):
                block = state_in[p, source, m].astype(F32)
                for half in range(2):
                    wide[half, pl.ds(source * SHARE + m, 4, stride=ENS), :] = block[
                        :, 128 * half : 128 * half + 128
                    ]
            return carry

        lax.fori_loop(0, GROUP, widen, 0)
        mix = trans[p]
        for level in range(4):
            for half in range(2):
                rows = slice(ENS * level, ENS * level + ENS)
                block = wide[half, rows, :]
                mean_state = jnp.mean(block, axis=0, keepdims=True)
                perturb = (block - mean_state).astype(BF16)
                mixed[half, rows, :] = (
                    jnp.dot(mix, perturb, preferred_element_type=F32) + mean_state
                )

        def narrow(step, carry):
            to = lax.rem(me + 5 * step, GROUP)
            for m in range(SHARE):
                block = jnp.concatenate(
                    [
                        mixed[half, pl.ds(to * SHARE + m, 4, stride=ENS), :]
                        for half in range(2)
                    ],
                    axis=1,
                )
                back[p, to, m] = block.astype(BF16)

            @pl.when(step > 0)
            def _():
                pltpu.make_async_remote_copy(
                    src_ref=back.at[p, to],
                    dst_ref=out.at[me * SHARE + p],
                    send_sem=back_send,
                    recv_sem=back_recv,
                    device_id={"mem": to},
                    device_id_type=MESH,
                ).start()

            @pl.when(step == 0)
            def _():
                pltpu.make_async_copy(
                    back.at[p, me], out.at[me * SHARE + p], back_own.at[p]
                ).start()

            return carry

        lax.fori_loop(0, GROUP, narrow, 0)
        return carry

    lax.fori_loop(0, SHARE, analyse, 0)

    others = (GROUP - 1) * SHARE
    msg_all.wait_send()
    for ref, send in ((state, state_send), (out, back_send)):
        whole = pltpu.make_async_remote_copy(
            src_ref=ref.at[pl.ds(0, others)],
            dst_ref=out.at[pl.ds(0, others)],
            send_sem=send,
            recv_sem=back_recv,
            device_id={"mem": lax.rem(me + 1, GROUP)},
            device_id_type=MESH,
        )
        whole.wait_send()
    whole.wait_recv()
    for p in range(SHARE):
        pltpu.make_async_copy(back.at[p, me], out.at[me * SHARE + p], back_own.at[p]).wait()


def body(state, obs_ens, obs_values, obs_index, patch_count, slot_weight):
    vmem, dma = pltpu.VMEM, pltpu.SemaphoreType.DMA
    block = state.shape[1:]
    scratch = [
        vmem(obs_ens.shape, F32),
        vmem(obs_values.shape, F32),
        vmem((8,) + obs_ens.shape[:3] + (RIM,), F32),
        vmem((8,) + obs_values.shape[:3] + (RIM,), F32),
        vmem(obs_index.shape, jnp.int32),
        vmem((SHARE, SLOTS), F32),
        vmem(patch_count.shape, jnp.int32),
        vmem((CHUNKS * 8, CHUNK), BF16),
        vmem((CHUNKS, CHUNK), F32),
        vmem((CHUNKS * 2, CHUNK), BF16),
        vmem((CHUNKS * 8, CHUNK), BF16),
        vmem((SHARE, SLOTS), F32),
        vmem((SHARE, SLOTS), F32),
        vmem((GROUP, MSG, SLOTS), BF16),
        vmem((GROUP, MSG, SLOTS), BF16),
        vmem((SHARE, GROUP) + block, BF16),
        vmem((SHARE, 2 * ENS, ENS), F32),
        vmem((SHARE, 8, SLOTS), F32),
        vmem((SHARE, 8, SLOTS), F32),
        vmem((SHARE, ENS, ENS), BF16),
        vmem((2, 4 * ENS, 128), F32),
        vmem((2, 4 * ENS, 128), F32),
        vmem((SHARE, GROUP) + block, BF16),
        dma((5,)),
        dma((8,)), dma((8,)), dma((8,)), dma((8,)),
        dma, dma, dma,
        dma, dma((SHARE,)), dma((SHARE,)),
        dma, dma, dma((SHARE,)),
    ]
    return pl.pallas_call(
        kernel,
        out_shape=jax.ShapeDtypeStruct(state.shape, state.dtype),
        in_specs=[pl.BlockSpec(memory_space=pl.ANY)] * 6,
        out_specs=pl.BlockSpec(memory_space=pl.ANY),
        scratch_shapes=scratch,
        compiler_params=pltpu.CompilerParams(
            collective_id=0, has_side_effects=True, vmem_limit_bytes=40 * 2**20
        ),
        name="letkf",
    )(state, obs_ens, obs_values, obs_index, patch_count, slot_weight)


def solution(mesh):
    placed = (
        P(("gx", "gy"), "mem", None, None),
        P("mem", "gx", "gy", None),
        P(None, "gx", "gy", None),
        P(("gx", "gy"), None),
        P(("gx", "gy")),
        P(("gx", "gy"), None),
    )
    return jax.shard_map(
        body,
        mesh=mesh,
        in_specs=placed,
        out_specs=P(("gx", "gy"), "mem", None, None),
        check_vma=False,
    )
```

time: 312 us -> 118 us (0.38)
  the two profiles are of different devices: /device:TPU:65 before, /device:TPU:1 now
where the time goes in v1:
time: 118 us; the launch traced here: 117 us
  Pallas kernels  110 us (93%)
  local copies, waits for them, and re-layouts  7.03 us (6%)
    pallas_call x1, Pallas kernels, body(): pl.pallas_call(kernel, out_shape=jax.ShapeDtypeStruct(state.shape, state....  110 us
    unnamed x13, local copies, waits for them, and re-layouts  7.03 us

profile of v1, /device:TPU:1, one launch (start us, length us, event | category | flops | bytes accessed | tf_op | source)
XLA Modules:
  0.0 117.5 jit_solution(13990679699008958428)
XLA Ops:
  0.0 0.0 copy-start
  0.0 1.6 %copy-done = bf16[128,8,4,256]{3,2,1,0:T(4,128)(2,1)S(1)} copy-done((bf16[128,8,4,256]{3,2,1,0:T(4,128)(2,1)S(1)}, bf16[128,8,4,256]{3,2,1,0:T(4,128)(2,1)}, u32[]{:S(2)}) %copy-start) | copy-done | bytes 2097176
  1.6 0.0 copy-start.1
  1.6 0.9 copy-done.1
  2.5 0.0 copy-start.2
  2.5 0.8 copy-done.2
  3.4 0.0 copy-start.3
  3.4 0.8 copy-done.3
  4.2 0.0 copy-start.4
  4.2 0.8 copy-done.4
  5.1 0.0 copy-start.5
  5.1 0.7 copy-done.5
  5.7 110.4 %letkf.1 = bf16[128,8,4,256]{3,2,1,0:T(4,128)(2,1)S(1)} custom-call(bf16[128,8,4,256]{3,2,1,0:T(4,128)(2,1)S(1)} %copy-done, f32[8,1,1,8192]{3,2,1,0:T(1,128)S(1)} %copy-done.1, f32[2,1,1,8192]{3,2,1,0:T(1,128)S(1)} %copy-done.2, s32[128,128]{1,0:T(8,128)S(1)} %copy-done.3, s32[128]{0:T(128)S(1)} %copy-done.5, f32[128,128]{1,0:T(8,128)S(1)} %copy-done.4), custom_call_target="tpu_custom_call" | custom-call | tf_op jit(solution)/shard_map/letkf/pallas_call | solution.py:458
  116.1 1.3 %copy.8 = bf16[128,8,4,256]{3,2,1,0:T(4,128)(2,1)} copy(bf16[128,8,4,256]{3,2,1,0:T(4,128)(2,1)S(1)} %letkf.1) | data formatting | bytes 4194304
Async XLA Ops:
  0.0 1.6 %copy-start = (bf16[128,8,4,256]{3,2,1,0:T(4,128)(2,1)S(1)}, bf16[128,8,4,256]{3,2,1,0:T(4,128)(2,1)}, u32[]{:S(2)}) copy-start(bf16[128,8,4,256]{3,2,1,0:T(4,128)(2,1)} %state.1) | copy-start | bytes 6291460
  1.6 0.9 copy-start.1
  2.5 0.8 copy-start.2
  3.4 0.8 copy-start.3
  4.2 0.8 copy-start.4
  5.1 0.7 copy-start.5

commit v2 on v1

--- a/solution.py
+++ b/solution.py
@@ -23,7 +23,8 @@
 OWN_CHUNKS = OBS // CHUNK
 RIM_CHUNKS = RIM // CHUNK
 CHUNKS = OWN_CHUNKS + 8 * RIM_CHUNKS
-MSG = SHARE * SHARE + 2 * SHARE
+MSG = SHARE + 1
+HOLD = 5
 EARLY = 3
 
 SIDES = [(dx, dy) for dx in (-1, 0, 1) for dy in (-1, 0, 1) if (dx, dy) != (0, 0)]
@@ -97,14 +98,12 @@
         }
 
     barrier = pltpu.get_barrier_semaphore()
-    for dx, dy in SIDES:
-        pl.semaphore_signal(barrier, inc=1, device_id=tile_at(dx, dy), device_id_type=MESH)
     for step in range(1, GROUP):
         pl.semaphore_signal(
             barrier, inc=1, device_id={"mem": lax.rem(me + step, GROUP)}, device_id_type=MESH
         )
-    for load in loads:
-        load.start()
+    for dx, dy in SIDES:
+        pl.semaphore_signal(barrier, inc=1, device_id=tile_at(dx, dy), device_id_type=MESH)
 
     def own_state(patch):
         return pltpu.make_async_copy(
@@ -126,9 +125,12 @@
 
         lax.fori_loop(1, GROUP, one, 0)
 
+    pl.semaphore_wait(barrier, len(SIDES) + GROUP - 1)
+    send_state(0)
+    for load in loads:
+        load.start()
     for patch in range(SHARE):
         own_state(patch).start()
-    pl.semaphore_wait(barrier, len(SIDES) + GROUP - 1)
 
     loads[0].wait()
     loads[1].wait()
@@ -150,11 +152,11 @@
             copy.start()
             rims.append(copy)
 
-    for patch in range(EARLY):
+    for patch in range(1, EARLY):
         send_state(patch)
 
     def fill(chunk_pair, ens_block, vals_block):
-        mean = jnp.mean(ens_block, axis=0, keepdims=True)
+        mean = jnp.mean(ens_block, axis=0, keepdims=True).astype(BF16).astype(F32)
         dev = ens_block - mean
         rows = pl.ds(pl.multiple_of(chunk_pair * 16, 16), 16)
         pool[rows, :] = jnp.concatenate([dev[:, :CHUNK], dev[:, CHUNK:]], axis=0).astype(BF16)
@@ -194,10 +196,7 @@
         return carry
 
     lax.fori_loop(0, 8 * RIM_CHUNKS // 2, fill_rim, 0)
-    means = mean_f[...]
-    mean_high, mean_low = split(means)
-    mean_pool[0:CHUNKS, :] = mean_high
-    mean_pool[CHUNKS : 2 * CHUNKS, :] = mean_low
+    mean_pool[...] = mean_f[...].astype(BF16)
 
     for load in loads[2:]:
         load.wait()
@@ -230,24 +229,19 @@
             )
             onehot = jnp.where(sub_iota == two(lane), 1.0, 0.0).astype(BF16)
             pairs.append((onehot, jnp.broadcast_to(two(chunk), (8, 2 * SLOTS))))
-        heads = ([], [])
+        heads = []
         for pair, (onehot, chunk_of) in enumerate(pairs):
             dev = pick(pool, chunk_of, onehot)
-            msg_out[step, 16 * pair : 16 * pair + 16, :] = jnp.concatenate(
-                [dev[:, :SLOTS], dev[:, SLOTS:]], axis=0
-            ).astype(BF16)
+            msg_out[step, 2 * pair] = dev[:, :SLOTS].astype(BF16)
+            msg_out[step, 2 * pair + 1] = dev[:, SLOTS:].astype(BF16)
             rows = jnp.dot(mean_pool[...], onehot, preferred_element_type=F32)
             turned = chunk_of - row_iota
-            for part in range(2):
-                found = jnp.zeros((8, 2 * SLOTS), F32)
-                for k in range(CHUNKS // 8):
-                    at = part * CHUNKS + 8 * k
-                    found = jnp.where(turned == 8 * k, rows[at : at + 8], found)
-                found = jnp.sum(found, axis=0, keepdims=True)
-                heads[part].extend([found[:, :SLOTS], found[:, SLOTS:]])
-        msg_out[step, SHARE * SHARE : MSG, :] = jnp.concatenate(
-            heads[0] + heads[1], axis=0
-        ).astype(BF16)
+            found = jnp.zeros((8, 2 * SLOTS), F32)
+            for k in range(CHUNKS // 8):
+                found = jnp.where(turned == 8 * k, rows[8 * k : 8 * k + 8], found)
+            found = jnp.sum(found, axis=0, keepdims=True)
+            heads.extend([found[:, :SLOTS], found[:, SLOTS:]])
+        msg_out[step, SHARE] = jnp.concatenate(heads, axis=0).astype(BF16)
 
         @pl.when(step < GROUP - 1)
         def _():
@@ -298,9 +292,8 @@
     lane_iota = lax.broadcasted_iota(jnp.int32, (1, SLOTS), 1)
     counts_row = counts_v[...].reshape(1, PATCHES).astype(F32)
     for p in range(SHARE):
-        dev = msg_in[:, SHARE * p : SHARE * p + SHARE, :].astype(F32)
-        heads = msg_in[:, SHARE * SHARE : MSG, :].astype(F32)
-        head = heads[:, p : p + 1, :] + heads[:, SHARE + p : SHARE + p + 1, :]
+        dev = msg_in[:, p].astype(F32)
+        head = msg_in[:, SHARE].astype(F32)[:, p : p + 1, :]
         chosen = (dev + head).reshape(ENS, SLOTS)
         mean_obs = jnp.mean(chosen, axis=0, keepdims=True)
         spread = chosen - mean_obs
@@ -381,7 +374,7 @@
                 )
                 back[p, to, m] = block.astype(BF16)
 
-            @pl.when(step > 0)
+            @pl.when((step > 0) & (p < HOLD))
             def _():
                 pltpu.make_async_remote_copy(
                     src_ref=back.at[p, to],
@@ -404,6 +397,30 @@
         return carry
 
     lax.fori_loop(0, SHARE, analyse, 0)
+
+    def rest(step, carry):
+        turn = step // 2
+        chip = jnp.where(turn < 4, turn, 4 + lax.rem(me // 2 + turn, 4))
+        to = chip * 2 + lax.rem(step, 2)
+
+        @pl.when(to != me)
+        def _():
+            def one(p, carry):
+                pltpu.make_async_remote_copy(
+                    src_ref=back.at[p, to],
+                    dst_ref=out.at[me * SHARE + p],
+                    send_sem=back_send,
+                    recv_sem=back_recv,
+                    device_id={"mem": to},
+                    device_id_type=MESH,
+                ).start()
+                return carry
+
+            lax.fori_loop(HOLD, SHARE, one, 0)
+
+        return carry
+
+    lax.fori_loop(0, GROUP, rest, 0)
 
     others = (GROUP - 1) * SHARE
     msg_all.wait_send()
@@ -435,12 +452,12 @@
         vmem(patch_count.shape, jnp.int32),
         vmem((CHUNKS * 8, CHUNK), BF16),
         vmem((CHUNKS, CHUNK), F32),
-        vmem((CHUNKS * 2, CHUNK), BF16),
+        vmem((CHUNKS, CHUNK), BF16),
         vmem((CHUNKS * 8, CHUNK), BF16),
         vmem((SHARE, SLOTS), F32),
         vmem((SHARE, SLOTS), F32),
-        vmem((GROUP, MSG, SLOTS), BF16),
-        vmem((GROUP, MSG, SLOTS), BF16),
+        vmem((GROUP, MSG, SHARE, SLOTS), BF16),
+        vmem((GROUP, MSG, SHARE, SLOTS), BF16),
         vmem((SHARE, GROUP) + block, BF16),
         vmem((SHARE, 2 * ENS, ENS), F32),
         vmem((SHARE, 8, SLOTS), F32),
@@ -457,15 +474,18 @@
     ]
     return pl.pallas_call(
         kernel,
-        out_shape=jax.ShapeDtypeStruct(state.shape, state.dtype),
+        out_shape=pltpu.VMEM(state.shape, state.dtype),
         in_specs=[pl.BlockSpec(memory_space=pl.ANY)] * 6,
-        out_specs=pl.BlockSpec(memory_space=pl.ANY),
+        out_specs=pl.BlockSpec(memory_space=pltpu.VMEM),
         scratch_shapes=scratch,
         compiler_params=pltpu.CompilerParams(
             collective_id=0, has_side_effects=True, vmem_limit_bytes=40 * 2**20
         ),
         name="letkf",
-    )(state, obs_ens, obs_values, obs_index, patch_count, slot_weight)
+    )(*[
+        pltpu.with_memory_space_constraint(a, pltpu.HBM)
+        for a in (state, obs_ens, obs_values, obs_index, patch_count, slot_weight)
+    ])
 
 
 def solution(mesh):

time: 118 us -> 109 us (0.924)
  the two profiles are of different devices: /device:TPU:1 before, /device:TPU:65 now
where the time goes in v2:
time: 109 us
  Pallas kernels  108 us (99%)
  local copies, waits for them, and re-layouts  1.32 us (1%)
    pallas_call x1, Pallas kernels, body(): pl.pallas_call(kernel, out_shape=pltpu.VMEM(state.shape, state.dtype), in...  108 us

profile of v2, /device:TPU:65, one launch (start us, length us, event | category | flops | bytes accessed | tf_op | source)
XLA Modules:
  0.0 109.3 jit_solution(15127402398848671670)
XLA Ops:
  0.0 107.9 %letkf.1 = bf16[128,8,4,256]{3,2,1,0:T(4,128)(2,1)S(1)} custom-call(bf16[128,8,4,256]{3,2,1,0:T(4,128)(2,1)} %state.1, f32[8,1,1,8192]{3,2,1,0:T(1,128)} %ens.1, f32[2,1,1,8192]{3,2,1,0:T(1,128)} %vals.1, s32[128,128]{1,0:T(8,128)} %index.1, s32[128]{0:T(128)} %counts.1, f32[128,128]{1,0:T(8,128)} %weights.1), custom_call_target="tpu_custom_call" | custom-call | tf_op jit(solution)/shard_map/letkf/pallas_call | solution.py:475
  108.0 1.3 %copy.8 = bf16[128,8,4,256]{3,2,1,0:T(4,128)(2,1)} copy(bf16[128,8,4,256]{3,2,1,0:T(4,128)(2,1)S(1)} %letkf.1) | data formatting | bytes 4194304

commit v3 on v2

--- a/solution.py
+++ b/solution.py
@@ -25,7 +25,7 @@
 CHUNKS = OWN_CHUNKS + 8 * RIM_CHUNKS
 MSG = SHARE + 1
 HOLD = 5
-EARLY = 3
+EARLY = 5
 
 SIDES = [(dx, dy) for dx in (-1, 0, 1) for dy in (-1, 0, 1) if (dx, dy) != (0, 0)]
 
@@ -74,7 +74,7 @@
     msg_out, msg_in, state_in, root, pulled_s, frob_s, trans, wide, mixed, back,
     local_sem, rim_send, rim_recv, val_send, val_recv,
     msg_send, msg_recv, msg_own, state_send, state_recv, state_own,
-    back_send, back_recv, back_own,
+    back_send, back_recv, back_own, ready, go,
 ):
     me = lax.axis_index("mem")
     tile_x = lax.axis_index("gx")
@@ -102,8 +102,10 @@
         pl.semaphore_signal(
             barrier, inc=1, device_id={"mem": lax.rem(me + step, GROUP)}, device_id_type=MESH
         )
-    for dx, dy in SIDES:
-        pl.semaphore_signal(barrier, inc=1, device_id=tile_at(dx, dy), device_id_type=MESH)
+    @pl.when(me == 0)
+    def _():
+        for dx, dy in SIDES:
+            pl.semaphore_signal(barrier, inc=1, device_id=tile_at(dx, dy), device_id_type=MESH)
 
     def own_state(patch):
         return pltpu.make_async_copy(
@@ -125,15 +127,57 @@
 
         lax.fori_loop(1, GROUP, one, 0)
 
-    pl.semaphore_wait(barrier, len(SIDES) + GROUP - 1)
+    pl.semaphore_wait(barrier, GROUP - 1 + jnp.where(me == 0, len(SIDES), 0))
     send_state(0)
     for load in loads:
         load.start()
     for patch in range(SHARE):
         own_state(patch).start()
 
+    for patch in range(1, EARLY):
+        send_state(patch)
+
+    @pl.when(me == 0)
+    def _():
+        for dx, dy in SIDES:
+            pl.semaphore_signal(ready, inc=1, device_id=tile_at(dx, dy), device_id_type=MESH)
+        pl.semaphore_wait(ready, len(SIDES))
+        for step in range(1, GROUP):
+            pl.semaphore_signal(go, inc=1, device_id={"mem": step}, device_id_type=MESH)
+
     loads[0].wait()
     loads[1].wait()
+
+    def fill(chunk_pair, ens_block, vals_block):
+        mean = jnp.mean(ens_block, axis=0, keepdims=True).astype(BF16).astype(F32)
+        dev = ens_block - mean
+        rows = pl.ds(pl.multiple_of(chunk_pair * 16, 16), 16)
+        pool[rows, :] = jnp.concatenate([dev[:, :CHUNK], dev[:, CHUNK:]], axis=0).astype(BF16)
+        mean_f[pl.ds(chunk_pair * 2, 1), :] = mean[:, :CHUNK]
+        mean_f[pl.ds(chunk_pair * 2 + 1, 1), :] = mean[:, CHUNK:]
+        first = vals_block.astype(BF16).astype(F32)
+        rest = vals_block - first
+        second = rest.astype(BF16).astype(F32)
+        parts = jnp.concatenate([first, second, rest - second, jnp.zeros_like(first)], axis=0)
+        val_pool[rows, :] = jnp.concatenate(
+            [parts[:, :CHUNK], parts[:, CHUNK:]], axis=0
+        ).astype(BF16)
+
+    def fill_own(pair, carry):
+        cols = pl.ds(pl.multiple_of(pair * 2 * CHUNK, 2 * CHUNK), 2 * CHUNK)
+        fill(
+            pair,
+            jnp.concatenate([ens_raw[m, 0, :, cols] for m in range(SHARE)], axis=0),
+            jnp.concatenate([vals_raw[c, 0, :, cols] for c in range(2)], axis=0),
+        )
+        return carry
+
+    lax.fori_loop(0, OWN_CHUNKS // 2, fill_own, 0)
+
+    @pl.when(me != 0)
+    def _():
+        pl.semaphore_wait(go, 1)
+
     rims = []
     for side, (dx, dy) in enumerate(SIDES):
         slot = len(SIDES) - 1 - side
@@ -151,35 +195,6 @@
             )
             copy.start()
             rims.append(copy)
-
-    for patch in range(1, EARLY):
-        send_state(patch)
-
-    def fill(chunk_pair, ens_block, vals_block):
-        mean = jnp.mean(ens_block, axis=0, keepdims=True).astype(BF16).astype(F32)
-        dev = ens_block - mean
-        rows = pl.ds(pl.multiple_of(chunk_pair * 16, 16), 16)
-        pool[rows, :] = jnp.concatenate([dev[:, :CHUNK], dev[:, CHUNK:]], axis=0).astype(BF16)
-        mean_f[pl.ds(chunk_pair * 2, 1), :] = mean[:, :CHUNK]
-        mean_f[pl.ds(chunk_pair * 2 + 1, 1), :] = mean[:, CHUNK:]
-        first = vals_block.astype(BF16).astype(F32)
-        rest = vals_block - first
-        second = rest.astype(BF16).astype(F32)
-        parts = jnp.concatenate([first, second, rest - second, jnp.zeros_like(first)], axis=0)
-        val_pool[rows, :] = jnp.concatenate(
-            [parts[:, :CHUNK], parts[:, CHUNK:]], axis=0
-        ).astype(BF16)
-
-    def fill_own(pair, carry):
-        cols = pl.ds(pl.multiple_of(pair * 2 * CHUNK, 2 * CHUNK), 2 * CHUNK)
-        fill(
-            pair,
-            jnp.concatenate([ens_raw[m, 0, :, cols] for m in range(SHARE)], axis=0),
-            jnp.concatenate([vals_raw[c, 0, :, cols] for c in range(2)], axis=0),
-        )
-        return carry
-
-    lax.fori_loop(0, OWN_CHUNKS // 2, fill_own, 0)
 
     for copy in rims:
         copy.wait()
@@ -471,6 +486,7 @@
         dma, dma, dma,
         dma, dma((SHARE,)), dma((SHARE,)),
         dma, dma, dma((SHARE,)),
+        pltpu.SemaphoreType.REGULAR, pltpu.SemaphoreType.REGULAR,
     ]
     return pl.pallas_call(
         kernel,

time: 109 us -> 106 us (0.972)
  Pallas kernels: 108 us -> 105 us
    pallas_call x1, Pallas kernels: 108 us -> 105 us  [body(): pl.pallas_call(kernel, out_shape=pltpu.VMEM(state.shape, state.dtype), in...]
where the time goes in v3:
time: 106 us
  Pallas kernels  105 us (99%)
  local copies, waits for them, and re-layouts  1.32 us (1%)
    pallas_call x1, Pallas kernels, body(): pl.pallas_call(kernel, out_shape=pltpu.VMEM(state.shape, state.dtype), in...  105 us

profile of v3, /device:TPU:65, one launch (start us, length us, event | category | flops | bytes accessed | tf_op | source)
XLA Modules:
  0.0 106.3 jit_solution(13796054582935147623)
XLA Ops:
  0.0 105.0 %letkf.1 = bf16[128,8,4,256]{3,2,1,0:T(4,128)(2,1)S(1)} custom-call(bf16[128,8,4,256]{3,2,1,0:T(4,128)(2,1)} %state.1, f32[8,1,1,8192]{3,2,1,0:T(1,128)} %ens.1, f32[2,1,1,8192]{3,2,1,0:T(1,128)} %vals.1, s32[128,128]{1,0:T(8,128)} %index.1, s32[128]{0:T(128)} %counts.1, f32[128,128]{1,0:T(8,128)} %weights.1), custom_call_target="tpu_custom_call" | custom-call | tf_op jit(solution)/shard_map/letkf/pallas_call | solution.py:491
  105.0 1.3 %copy.8 = bf16[128,8,4,256]{3,2,1,0:T(4,128)(2,1)} copy(bf16[128,8,4,256]{3,2,1,0:T(4,128)(2,1)S(1)} %letkf.1) | data formatting | bytes 4194304

commit v4 on v3

--- a/solution.py
+++ b/solution.py
@@ -134,8 +134,7 @@
     for patch in range(SHARE):
         own_state(patch).start()
 
-    for patch in range(1, EARLY):
-        send_state(patch)
+    send_state(1)
 
     @pl.when(me == 0)
     def _():
@@ -195,6 +194,9 @@
             )
             copy.start()
             rims.append(copy)
+
+    for patch in range(2, EARLY):
+        send_state(patch)
 
     for copy in rims:
         copy.wait()

time: 106 us -> 106 us (level)
  no operation moved by 1% of the time
where the time goes in v4:
time: 106 us
  Pallas kernels  105 us (99%)
  local copies, waits for them, and re-layouts  1.32 us (1%)
    pallas_call x1, Pallas kernels, body(): pl.pallas_call(kernel, out_shape=pltpu.VMEM(state.shape, state.dtype), in...  105 us

profile of v4, /device:TPU:65, one launch (start us, length us, event | category | flops | bytes accessed | tf_op | source)
XLA Modules:
  0.0 106.3 jit_solution(8396761490990089070)
XLA Ops:
  0.0 105.0 %letkf.1 = bf16[128,8,4,256]{3,2,1,0:T(4,128)(2,1)S(1)} custom-call(bf16[128,8,4,256]{3,2,1,0:T(4,128)(2,1)} %state.1, f32[8,1,1,8192]{3,2,1,0:T(1,128)} %ens.1, f32[2,1,1,8192]{3,2,1,0:T(1,128)} %vals.1, s32[128,128]{1,0:T(8,128)} %index.1, s32[128]{0:T(128)} %counts.1, f32[128,128]{1,0:T(8,128)} %weights.1), custom_call_target="tpu_custom_call" | custom-call | tf_op jit(solution)/shard_map/letkf/pallas_call | solution.py:493
  105.0 1.3 %copy.8 = bf16[128,8,4,256]{3,2,1,0:T(4,128)(2,1)} copy(bf16[128,8,4,256]{3,2,1,0:T(4,128)(2,1)S(1)} %letkf.1) | data formatting | bytes 4194304

commit v5 on v4

--- a/solution.py
+++ b/solution.py
@@ -418,7 +418,7 @@
     def rest(step, carry):
         turn = step // 2
         chip = jnp.where(turn < 4, turn, 4 + lax.rem(me // 2 + turn, 4))
-        to = chip * 2 + lax.rem(step, 2)
+        to = chip * 2 + 1 - lax.rem(step, 2)
 
         @pl.when(to != me)
         def _():

time: 106 us -> 106 us (level)
  no operation moved by 1% of the time
where the time goes in v5:
time: 106 us
  Pallas kernels  104 us (98%)
  local copies, waits for them, and re-layouts  1.32 us (1%)
    pallas_call x1, Pallas kernels, body(): pl.pallas_call(kernel, out_shape=pltpu.VMEM(state.shape, state.dtype), in...  104 us

profile of v5, /device:TPU:65, one launch (start us, length us, event | category | flops | bytes accessed | tf_op | source)
XLA Modules:
  0.0 105.5 jit_solution(186392253402975485)
XLA Ops:
  0.0 104.2 %letkf.1 = bf16[128,8,4,256]{3,2,1,0:T(4,128)(2,1)S(1)} custom-call(bf16[128,8,4,256]{3,2,1,0:T(4,128)(2,1)} %state.1, f32[8,1,1,8192]{3,2,1,0:T(1,128)} %ens.1, f32[2,1,1,8192]{3,2,1,0:T(1,128)} %vals.1, s32[128,128]{1,0:T(8,128)} %index.1, s32[128]{0:T(128)} %counts.1, f32[128,128]{1,0:T(8,128)} %weights.1), custom_call_target="tpu_custom_call" | custom-call | tf_op jit(solution)/shard_map/letkf/pallas_call | solution.py:493
  104.2 1.3 %copy.8 = bf16[128,8,4,256]{3,2,1,0:T(4,128)(2,1)} copy(bf16[128,8,4,256]{3,2,1,0:T(4,128)(2,1)S(1)} %letkf.1) | data formatting | bytes 4194304

commit v6 on v5

--- a/solution.py
+++ b/solution.py
@@ -415,14 +415,16 @@
 
     lax.fori_loop(0, SHARE, analyse, 0)
 
-    def rest(step, carry):
-        turn = step // 2
-        chip = jnp.where(turn < 4, turn, 4 + lax.rem(me // 2 + turn, 4))
-        to = chip * 2 + 1 - lax.rem(step, 2)
-
-        @pl.when(to != me)
-        def _():
-            def one(p, carry):
+    def rest(turn, carry):
+        mine = me // 2
+        chip = jnp.where(turn < 4, turn, 4 + lax.rem(mine + turn, 4))
+
+        def one(k, carry):
+            p = HOLD + k // 2
+            to = chip * 2 + 1 - lax.rem(k, 2)
+
+            @pl.when(to != me)
+            def _():
                 pltpu.make_async_remote_copy(
                     src_ref=back.at[p, to],
                     dst_ref=out.at[me * SHARE + p],
@@ -431,13 +433,13 @@
                     device_id={"mem": to},
                     device_id_type=MESH,
                 ).start()
-                return carry
-
-            lax.fori_loop(HOLD, SHARE, one, 0)
-
+
+            return carry
+
+        lax.fori_loop(0, 2 * (SHARE - HOLD), one, 0)
         return carry
 
-    lax.fori_loop(0, GROUP, rest, 0)
+    lax.fori_loop(0, GROUP // 2, rest, 0)
 
     others = (GROUP - 1) * SHARE
     msg_all.wait_send()

time: 106 us -> 106 us (level)
  no operation moved by 1% of the time
where the time goes in v6:
time: 106 us
  Pallas kernels  105 us (99%)
  local copies, waits for them, and re-layouts  1.32 us (1%)
    pallas_call x1, Pallas kernels, body(): pl.pallas_call(kernel, out_shape=pltpu.VMEM(state.shape, state.dtype), in...  105 us

profile of v6, /device:TPU:65, one launch (start us, length us, event | category | flops | bytes accessed | tf_op | source)
XLA Modules:
  0.0 106.2 jit_solution(15444040736140534474)
XLA Ops:
  0.0 104.9 %letkf.1 = bf16[128,8,4,256]{3,2,1,0:T(4,128)(2,1)S(1)} custom-call(bf16[128,8,4,256]{3,2,1,0:T(4,128)(2,1)} %state.1, f32[8,1,1,8192]{3,2,1,0:T(1,128)} %ens.1, f32[2,1,1,8192]{3,2,1,0:T(1,128)} %vals.1, s32[128,128]{1,0:T(8,128)} %index.1, s32[128]{0:T(128)} %counts.1, f32[128,128]{1,0:T(8,128)} %weights.1), custom_call_target="tpu_custom_call" | custom-call | tf_op jit(solution)/shard_map/letkf/pallas_call | solution.py:495
  104.9 1.3 %copy.8 = bf16[128,8,4,256]{3,2,1,0:T(4,128)(2,1)} copy(bf16[128,8,4,256]{3,2,1,0:T(4,128)(2,1)S(1)} %letkf.1) | data formatting | bytes 4194304
